TPU v7x, 256 devices: a whole 4x4x8 slice. The times are simulated.
256 devices in a mesh: ctx: 16 (over z, core), head: 16 (over x, y).
Axes of the slice: x: 4, y: 4, z: 8, core: 2. Of those that a mesh axis runs over, the one named last changes fastest.
Arguments:
- query_states: bfloat16 [8192, 8192], P('ctx', 'head'), may hold values from -8 to 8
- key_states: bfloat16 [8192, 1024], P('ctx'), may hold values from -8 to 8
- value_states: bfloat16 [8192, 1024], P('ctx'), may hold values from -6 to 6
- out_grad: bfloat16 [8192, 8192], P('ctx', 'head'), may hold values from -6 to 6
- stretch_order: int32 [64], replicated, may hold values from 0 to 63, each once
- doc_blocks: int32 [16], replicated, may hold values from 1 to 8, 64 in all
Outputs:
- attention_out: bfloat16 [8192, 8192], P('ctx', 'head')
- query_grad: bfloat16 [8192, 8192], P(('ctx', 'head'))
- key_grad: bfloat16 [8192, 1024], P(('ctx', 'head'))
- value_grad: bfloat16 [8192, 1024], P(('ctx', 'head'))
Inputs may be any that keep to these rules, and one draw needn't show every extreme that they name: `doc_blocks`: each document spans 1 to 8 stretches.
All inputs are finite; a program needn't handle non-finite values.
Results may differ from a plain program's by a relative error of at most 0.035.
Values may be sent and summed in bfloat16 or wider, within the bound.
A program may use at most 128 MiB of HBM per device.

v0:
```python
import math

import jax
import jax.numpy as jnp
from jax import lax
from jax.sharding import PartitionSpec as P

QHEADS = 64
KVHEADS = 8
HD = 128
STRETCH = 128


masked_value = -1e30


def stretch_of_slot(stretch_order, slot_ids):
    table = jnp.arange(stretch_order.shape[0], dtype=jnp.int32)
    return jnp.sum(jnp.where(slot_ids[..., None] == table, stretch_order, 0), axis=-1)


def doc_numbers(positions, doc_ends):
    return jnp.sum((positions[..., None] >= doc_ends).astype(jnp.int32), axis=-1)


def on_device(query_states, key_states, value_states, out_grad, stretch_order, doc_blocks):
    row_count = query_states.shape[0]
    head_count = lax.axis_size("head")
    head_index = lax.axis_index("head")
    ctx_index = lax.axis_index("ctx")
    q_local = query_states.shape[1] // HD
    group_size = QHEADS // KVHEADS
    kv_local = max(1, q_local // group_size)
    sharing = max(1, group_size // q_local)
    per_kv = q_local // kv_local
    stretch_total = stretch_order.shape[0]
    longest_doc = min(8, stretch_total // 2)
    seq_total = stretch_total * STRETCH
    scale_factor = HD ** (-0.5)
    first_kv = head_index * q_local // group_size
    key_mine = lax.dynamic_slice_in_dim(key_states, first_kv * HD, kv_local * HD, 1)
    value_mine = lax.dynamic_slice_in_dim(value_states, first_kv * HD, kv_local * HD, 1)
    doc_ends = jnp.cumsum(doc_blocks) * STRETCH
    table = jnp.arange(stretch_total, dtype=jnp.int32)
    slot_lookup = jnp.sum(
        jnp.where(stretch_order[None, :] == table[:, None], table[None, :], 0), axis=1
    )
    local_stretches = row_count // STRETCH
    own_slots = ctx_index * local_stretches + jnp.arange(local_stretches, dtype=jnp.int32)
    own_stretches = stretch_of_slot(stretch_order, own_slots)
    offsets = jnp.arange(longest_doc, dtype=jnp.int32)
    reach_stretch = own_stretches[:, None] - longest_doc + 1 + offsets[None, :]
    reach_valid = reach_stretch >= 0
    reach_clamp = jnp.maximum(reach_stretch, 0)
    reach_slot = jnp.sum(jnp.where(reach_clamp[..., None] == table, slot_lookup, 0), axis=-1)
    within = jnp.arange(STRETCH, dtype=jnp.int32)
    reach_rows = longest_doc * STRETCH
    query_pos = own_stretches[:, None] * STRETCH + within[None, :]
    key_pos = (reach_stretch[:, :, None] * STRETCH + within[None, None, :]).reshape(
        local_stretches, reach_rows
    )
    key_valid = jnp.broadcast_to(
        reach_valid[:, :, None], (local_stretches, longest_doc, STRETCH)
    ).reshape(local_stretches, reach_rows)
    allowed = (
        (doc_numbers(query_pos, doc_ends)[:, :, None] == doc_numbers(key_pos, doc_ends)[:, None, :])
        & (key_pos[:, None, :] <= query_pos[:, :, None])
        & key_valid[:, None, :]
    )
    whole_keys, whole_values = (
        lax.all_gather(key_mine, "ctx", axis=0, tiled=True),
        lax.all_gather(value_mine, "ctx", axis=0, tiled=True),
    )
    key_extent = whole_keys.reshape(stretch_total, STRETCH, kv_local, HD)[reach_slot].reshape(
        local_stretches, reach_rows, kv_local, HD
    )
    value_extent = whole_values.reshape(stretch_total, STRETCH, kv_local, HD)[reach_slot].reshape(
        local_stretches, reach_rows, kv_local, HD
    )
    query_heads = query_states.reshape(local_stretches, STRETCH, kv_local, per_kv, HD)
    grad_heads = out_grad.reshape(local_stretches, STRETCH, kv_local, per_kv, HD)
    group_stretches = math.gcd(local_stretches, max(1, 512 // STRETCH))
    step_count = local_stretches // group_stretches

    def by_step(array):
        return array.reshape((step_count, group_stretches) + array.shape[1:])

    def attend(carry, item):
        query_block, grad_block, key_block, value_block, allowed_block = item
        mask = allowed_block[:, None, None]
        logit_scores = (
            jnp.einsum(
                "cqgjd,ckgd->cgjqk", query_block, key_block, preferred_element_type=jnp.float32
            )
            * scale_factor
        )
        logit_scores = jnp.where(mask, logit_scores, masked_value)
        row_max = jnp.max(logit_scores, axis=-1)
        totals = jnp.sum(jnp.where(mask, jnp.exp(logit_scores - row_max[..., None]), 0.0), axis=-1)
        log_total = row_max + jnp.log(totals)
        weights = jnp.where(mask, jnp.exp(logit_scores - log_total[..., None]), 0.0)
        weights_blocked = weights.astype(jnp.bfloat16)
        out_block = jnp.einsum(
            "cgjqk,ckgd->cqgjd", weights_blocked, value_block, preferred_element_type=jnp.float32
        ).astype(jnp.bfloat16)
        row_dots = jnp.sum(grad_block.astype(jnp.float32) * out_block.astype(jnp.float32), axis=-1)
        weight_gradient = jnp.einsum(
            "cqgjd,ckgd->cgjqk", grad_block, value_block, preferred_element_type=jnp.float32
        )
        score_gradient = (
            weights * (weight_gradient - row_dots.transpose(0, 2, 3, 1)[..., None])
        ).astype(jnp.bfloat16)
        query_portion = (
            jnp.einsum(
                "cgjqk,ckgd->cqgjd", score_gradient, key_block, preferred_element_type=jnp.float32
            )
            * scale_factor
        ).astype(jnp.bfloat16)
        key_portion = jnp.einsum(
            "cgjqk,cqgjd->ckgd", score_gradient, query_block, preferred_element_type=jnp.float32
        )
        value_portion = jnp.einsum(
            "cgjqk,cqgjd->ckgd", weights_blocked, grad_block, preferred_element_type=jnp.float32
        )
        return (carry, (out_block, query_portion, key_portion, value_portion))

    _unused, produced = lax.scan(
        attend,
        jnp.zeros((), jnp.float32),
        (
            by_step(query_heads),
            by_step(grad_heads),
            by_step(key_extent),
            by_step(value_extent),
            by_step(allowed),
        ),
    )
    out_steps, query_steps, key_steps, value_steps = produced
    attention_out = out_steps.reshape(row_count, q_local * HD)
    query_local = query_steps.reshape(row_count, q_local * HD)
    flat_slots = reach_slot.reshape(-1)
    key_acc = (
        jnp.zeros((stretch_total, STRETCH, kv_local, HD), jnp.float32)
        .at[flat_slots]
        .add(key_steps.reshape(local_stretches * longest_doc, STRETCH, kv_local, HD))
        .reshape(seq_total, kv_local, HD)
    )
    value_acc = (
        jnp.zeros((stretch_total, STRETCH, kv_local, HD), jnp.float32)
        .at[flat_slots]
        .add(value_steps.reshape(local_stretches * longest_doc, STRETCH, kv_local, HD))
        .reshape(seq_total, kv_local, HD)
    )
    query_grad = lax.all_to_all(query_local, "head", split_axis=0, concat_axis=1, tiled=True)
    stacked = jnp.stack([key_acc * scale_factor, value_acc], axis=1).reshape(
        seq_total, 2 * kv_local * HD
    )
    short_rows = row_count // head_count
    reduced = lax.psum_scatter(
        stacked.astype(jnp.bfloat16), "ctx", scatter_dimension=0, tiled=True
    ).astype(jnp.float32)
    arrived = lax.all_to_all(
        reduced.astype(jnp.bfloat16), "head", split_axis=0, concat_axis=1, tiled=True
    ).astype(reduced.dtype)
    regrouped = arrived.reshape(short_rows, head_count // sharing, sharing, 2, kv_local, HD).sum(
        axis=2
    )
    key_grad = regrouped[:, :, 0].reshape(short_rows, KVHEADS * HD).astype(jnp.bfloat16)
    value_grad = regrouped[:, :, 1].reshape(short_rows, KVHEADS * HD).astype(jnp.bfloat16)
    return (attention_out, query_grad, key_grad, value_grad)


def solution(mesh):
    in_specs = (P("ctx", "head"), P("ctx", None), P("ctx", None), P("ctx", "head"), P(), P())
    out_specs = (
        P("ctx", "head"),
        P(("ctx", "head"), None),
        P(("ctx", "head"), None),
        P(("ctx", "head"), None),
    )
    return jax.shard_map(
        on_device, mesh=mesh, in_specs=in_specs, out_specs=out_specs, check_vma=False
    )
```

profile of v0, /device:TPU:8, one launch (start us, length us, event | category | flops | bytes accessed | tf_op | source)
XLA Modules:
  0.0 231.8 jit_solution(8391017988952747926)
XLA Ops:
  17.2 2.3 and_and_fusion
  19.5 33.0 %all-gather.3.cloned.1.call-done = bf16[8192,128]{1,0:T(8,128)(2,1)} async-done(((bf16[512,128]{1,0:T(8,128)(2,1)}), bf16[8192,128]{1,0:T(8,128)(2,1)}) %all-gather.3.cloned.1.call-update) | async-done | bytes 2097168 | tf_op jit(solution)/shard_map/all_gather | solution.py:72
  52.5 3.3 %gather_fusion = bf16[32,128,128]{2,1,0:T(8,128)(2,1)} fusion(bf16[64,128,128]{2,1,0:T(8,128)(2,1)} %bitcast.160, s32[1024]{0:T(1024)S(1)} %pad_clamp_fusion), kind=kCustom, calls=%fused_computation | custom fusion | bytes 2097280 | tf_op jit(solution)/shard_map/gather | solution.py:77
  55.8 36.6 %all-gather.5.cloned.1.call-done = bf16[8192,128]{1,0:T(8,128)(2,1)} async-done(((bf16[512,128]{1,0:T(8,128)(2,1)}), bf16[8192,128]{1,0:T(8,128)(2,1)}) %all-gather.5.cloned.1.call-update) | async-done | bytes 2097168 | tf_op jit(solution)/shard_map/all_gather | solution.py:71
  92.4 2.3 %gather_fusion.1 = bf16[32,128,128]{2,1,0:T(8,128)(2,1)S(1)} fusion(bf16[64,128,128]{2,1,0:T(8,128)(2,1)} %bitcast.161, s32[1024]{0:T(1024)S(1)} %pad_clamp_fusion), kind=kCustom, calls=%fused_computation.1 | custom fusion | bytes 2097280 | tf_op jit(solution)/shard_map/gather | solution.py:74
  96.1 2.1 select_reduce_fusion
  98.3 3.7 %fusion.9 = f32[4,1024,128,1]{2,1,3,0:T(8,128)S(1)} fusion(bf16[4,128,4,128]{3,2,1,0:T(4,128)(2,1)S(1)} %copy-done.9, f32[4,1024,128,4]{2,1,3,0:T(8,128)S(1)} %get-tuple-element.41, f32[4,4,128]{2,1,0:T(4,128)S(1)} %bitcast.169, pred[4,128,1024]{1,2,0:T(8,128)(4,1)} %copy-done.3), kind=kOutput, calls=%fused_computation.25 | convolution fusion | flops 547356672 | bytes 11542528 | tf_op jit(solution)/shard_map/while/body/eval_jaxpr/cgjqk,cqgjd->ckgd/dot_general | solution.py:122
  102.0 2.9 %multiply_reduce_fusion = (f32[4,128,4]{1,2,0:T(4,128)S(1)}, bf16[4,128,1,4,128]{1,4,3,0,2:T(8,128)(2,1)}) fusion(f32[4,128,1,4,128]{1,4,3,0,2:T(8,128)S(1)} %copy-done.7, bf16[4,1024,128,1]{2,1,3,0:T(8,128)(2,1)S(1)} %bitcast.158, f32[4,1024,128,4]{2,1,3,0:T(8,128)S(1)} %get-tuple-element.41, f32[4,4,128]{2,1,0:T(4,128)S(1)} %bitcast.170, ...), kind=kOutput, calls=%fused_computation.22 | convolution fusion | flops 548403200 | bytes 11550720 | tf_op jit(solution)/shard_map/while/body/eval_jaxpr/cgjqk,ckgd->cqgjd/dot_general | solution.py:103
  104.9 4.3 %fusion.5 = bf16[4,4,128,1024]{2,3,1,0:T(8,128)(2,1)} fusion(f32[4,1024,128,4]{2,1,3,0:T(8,128)S(1)} %get-tuple-element.41, f32[4,4,128]{2,1,0:T(4,128)S(1)} %bitcast.173, f32[4,4,128]{2,1,0:T(4,128)S(1)} %bitcast.171, pred[4,128,1024]{1,2,0:T(8,128)(4,1)S(1)} %copy-done.4, bf16[4,1024,128,1]{2,1,3,0:T(8,128)(2,1)S(1)} %bitcast.159, ...), kind=kOutput, calls=%fused_computation.13 | convolution fusion | flops 551550976 | bytes 14696448 | tf_op jit(solution)/shard_map/while/body/eval_jaxpr/cqgjd,ckgd->cgjqk/dot_general | solution.py:107
  109.2 2.5 %broadcast.203.clone = f32[64,128,128]{2,1,0:T(8,128)} broadcast(f32[]{:T(128)} %constant.81.clone.1), dimensions={} | broadcast | bytes 4194308 | tf_op jit(solution)/shard_map/broadcast.17
  111.7 6.1 %scatter_fusion.1 = f32[64,128,128]{2,1,0:T(8,128)} fusion(f32[64,128,128]{2,1,0:T(8,128)} %broadcast.203.clone, s32[32]{0:T(128)S(1)} %fusion.19, f32[32,128,128]{2,1,0:T(8,128)S(1)} %bitcast.154), kind=kCustom, calls=%fused_computation.3 | custom fusion | flops 524288 | bytes 6291584 | tf_op jit(solution)/shard_map/scatter-add | solution.py:151
  117.8 2.6 %convert.19 = bf16[64,128,128]{2,1,0:T(8,128)(2,1)S(1)} convert(f32[64,128,128]{2,1,0:T(8,128)} %scatter_fusion.1) | non-fusion elementwise | flops 1048576 | bytes 6291456 | tf_op jit(solution)/shard_map/convert.7
  120.4 3.0 %copy.95 = bf16[8192,1,1,128]{0,3,1,2:T(8,128)(2,1)} copy(bf16[8192,1,1,128]{3,0,2,1:T(8,128)(2,1)S(1)} %bitcast.150) | data formatting | bytes 4194304 | tf_op jit(solution)/shard_map/stack;reshape | solution.py:155
  123.4 3.6 %fusion.12 = f32[4,1024,128,1]{2,1,3,0:T(8,128)S(1)} fusion(bf16[4,4,128,1024]{2,3,1,0:T(8,128)(2,1)} %fusion.5, bf16[4,128,4,128]{3,2,1,0:T(4,128)(2,1)} %copy-done.5), kind=kOutput, calls=%fused_computation.28 | convolution fusion | flops 536870912 | bytes 6815744 | tf_op jit(solution)/shard_map/while/body/eval_jaxpr/cgjqk,cqgjd->ckgd/dot_general | solution.py:119
  126.9 2.5 %broadcast.203.clone.1 = f32[64,128,128]{2,1,0:T(8,128)} broadcast(f32[]{:T(128)} %constant.81.clone.1), dimensions={} | broadcast | bytes 4194308 | tf_op jit(solution)/shard_map/broadcast.17
  129.4 6.1 %scatter_fusion = f32[64,128,128]{2,1,0:T(8,128)} fusion(f32[64,128,128]{2,1,0:T(8,128)} %broadcast.203.clone.1, s32[32]{0:T(128)S(1)} %fusion.19, f32[32,128,128]{2,1,0:T(8,128)S(1)} %bitcast.149), kind=kCustom, calls=%fused_computation.2 | custom fusion | flops 524288 | bytes 6291584 | tf_op jit(solution)/shard_map/scatter-add | solution.py:145
  135.5 2.8 %multiply_convert_fusion = bf16[64,128,128]{2,1,0:T(8,128)(2,1)S(1)} fusion(f32[64,128,128]{2,1,0:T(8,128)} %scatter_fusion), kind=kLoop, calls=%fused_computation.15 | loop fusion | flops 2097152 | bytes 6291456 | tf_op jit(solution)/shard_map/convert.8
  138.3 2.9 %copy.94 = bf16[8192,1,1,128]{0,3,1,2:T(8,128)(2,1)} copy(bf16[8192,1,1,128]{3,0,2,1:T(8,128)(2,1)S(1)} %bitcast.151) | data formatting | bytes 4194304 | tf_op jit(solution)/shard_map/mul | solution.py:155
  141.3 4.6 %pad_maximum_fusion = bf16[8192,2,1,128]{0,3,1,2:T(8,128)(2,1)} fusion(bf16[8192,1,1,128]{0,3,1,2:T(8,128)(2,1)} %copy.95, bf16[8192,1,1,128]{0,3,1,2:T(8,128)(2,1)} %copy.94), kind=kLoop, calls=%fused_computation.14 | loop fusion | flops 2097152 | bytes 8388608 | tf_op jit(solution)/shard_map/stack | solution.py:155
  147.1 3.0 %fusion.7 = bf16[4,128,1,4,128]{1,4,3,0,2:T(8,128)(2,1)S(1)} fusion(bf16[4,1024,128,1]{2,1,3,0:T(8,128)(2,1)S(1)} %bitcast.153, bf16[4,4,128,1024]{2,3,1,0:T(8,128)(2,1)} %fusion.5), kind=kOutput, calls=%fused_computation.20 | convolution fusion | flops 537395200 | bytes 5767168 | tf_op jit(solution)/shard_map/while/body/eval_jaxpr/cgjqk,ckgd->cqgjd/dot_general | solution.py:114
  151.4 7.3 %all-to-all-start = ((bf16[16,32,512]{2,1,0:T(8,128)(2,1)}), bf16[16,32,512]{2,1,0:T(8,128)(2,1)S(1)}, u32[]{:S(2)}, u32[]{:S(2)}) async-start(bf16[16,32,512]{2,1,0:T(8,128)(2,1)} %all_to_all.24), calls=%async_computation | async-start | bytes 1048576 | tf_op jit(solution)/shard_map/all_to_all | solution.py:154
  158.7 48.9 %reduce-scatter.2.cloned.1.call-done = bf16[512,256]{0,1:T(8,128)(2,1)} async-done(((bf16[8192,256]{0,1:T(8,128)(2,1)}), bf16[512,256]{0,1:T(8,128)(2,1)}) %reduce-scatter.2.cloned.1.call-update) | async-done | bytes 262160 | tf_op jit(solution)/shard_map/reduce_scatter | solution.py:159
  209.4 7.1 %all-to-all-start.1 = ((bf16[16,32,256]{2,1,0:T(8,128)(2,1)}), bf16[16,32,256]{2,1,0:T(8,128)(2,1)S(1)}, u32[]{:S(2)}, u32[]{:S(2)}) async-start(bf16[16,32,256]{2,1,0:T(8,128)(2,1)} %bitcast.44), calls=%async_computation.2 | async-start | bytes 524288 | tf_op jit(solution)/shard_map/all_to_all | solution.py:162
  218.5 4.9 %all-to-all-done.1 = bf16[16,32,256]{2,1,0:T(8,128)(2,1)S(1)} async-done(((bf16[16,32,256]{2,1,0:T(8,128)(2,1)}), bf16[16,32,256]{2,1,0:T(8,128)(2,1)S(1)}, u32[]{:S(2)}, u32[]{:S(2)}) %all-to-all-start.1) | async-done | bytes 262176 | tf_op jit(solution)/shard_map/all_to_all | solution.py:162
  (77 shorter events, 19.3 us)
Async XLA Ops:
  7.2 1.2 copy-start
  7.2 8.3 %copy-start.12 = (s32[64]{0:T(128)S(1)}, s32[64]{0:T(128)}, u32[]{:S(2)}) copy-start(s32[64]{0:T(128)} %param.10) | copy-start | bytes 772
  7.2 9.0 %copy-start.11 = (s32[16]{0:T(128)S(1)}, s32[16]{0:T(128)}, u32[]{:S(2)}) copy-start(s32[16]{0:T(128)} %param.11) | copy-start | bytes 196
  7.2 9.3 %copy-start.8 = (bf16[512,512]{1,0:T(8,128)(2,1)S(1)}, bf16[512,512]{1,0:T(8,128)(2,1)}, u32[]{:S(2)}) copy-start(bf16[512,512]{1,0:T(8,128)(2,1)} %param.6) | copy-start | bytes 1572868
  7.2 45.3 %all-gather.3.cloned.1.call-start = ((), (), s32[]{:S(2)}) async-start(), calls=%async_computation.3 | async-start | bytes 2228224 | tf_op jit(solution)/shard_map/all_gather | solution.py:72
  9.1 83.3 %all-gather.5.cloned.1.call-start = ((), (), s32[]{:S(2)}) async-start(), calls=%async_computation.4 | async-start | bytes 2228224 | tf_op jit(solution)/shard_map/all_gather | solution.py:71
  10.7 196.9 %reduce-scatter.2.cloned.1.call-start = ((), (), s32[]{:S(2)}) async-start(), calls=%async_computation.5 | async-start | bytes 4456448 | tf_op jit(solution)/shard_map/reduce_scatter | solution.py:159
  16.7 79.4 %copy-start.5 = (bf16[4,128,4,128]{3,2,1,0:T(4,128)(2,1)}, bf16[4,128,4,128]{3,2,1,0:T(4,128)(2,1)S(1)}, u32[]{:S(2)}) copy-start(bf16[4,128,4,128]{3,2,1,0:T(4,128)(2,1)S(1)} %reshape.365) | copy-start | bytes 1572868
  19.5 76.6 %copy-start.3 = (pred[4,128,1024]{1,2,0:T(8,128)(4,1)}, pred[4,128,1024]{1,2,0:T(8,128)(4,1)S(1)}, u32[]{:S(2)}) copy-start(pred[4,128,1024]{1,2,0:T(8,128)(4,1)S(1)} %and_and_fusion) | copy-start | bytes 1572868
  94.8 1.3 copy-start.1
  96.1 2.1 copy-start.9
  98.2 3.8 %copy-start.4 = (pred[4,128,1024]{1,2,0:T(8,128)(4,1)S(1)}, pred[4,128,1024]{1,2,0:T(8,128)(4,1)}, u32[]{:S(2)}) copy-start(pred[4,128,1024]{1,2,0:T(8,128)(4,1)} %copy-done.3) | copy-start | bytes 1572868
  98.2 3.8 %copy-start.6 = (bf16[32,128,128]{2,1,0:T(8,128)(2,1)S(1)}, bf16[32,128,128]{2,1,0:T(8,128)(2,1)}, u32[]{:S(2)}) copy-start(bf16[32,128,128]{2,1,0:T(8,128)(2,1)} %gather_fusion) | copy-start | bytes 3145732
  98.2 3.8 %copy-start.7 = (f32[4,128,1,4,128]{1,4,3,0,2:T(8,128)S(1)}, f32[4,128,1,4,128]{1,4,3,0,2:T(8,128)}, u32[]{:S(2)}) copy-start(f32[4,128,1,4,128]{1,4,3,0,2:T(8,128)} %copy.87) | copy-start | bytes 3145732
  145.8 1.2 copy-start.2
  147.1 69.4 %copy-start.10 = (bf16[4,128,1,4,128]{1,4,3,0,2:T(8,128)(2,1)S(1)}, bf16[4,128,1,4,128]{1,4,3,0,2:T(8,128)(2,1)}, u32[]{:S(2)}) copy-start(bf16[4,128,1,4,128]{1,4,3,0,2:T(8,128)(2,1)} %get-tuple-element.43) | copy-start | bytes 1572868
  151.4 58.0 %all-to-all-start = ((bf16[16,32,512]{2,1,0:T(8,128)(2,1)}), bf16[16,32,512]{2,1,0:T(8,128)(2,1)S(1)}, u32[]{:S(2)}, u32[]{:S(2)}) async-start(bf16[16,32,512]{2,1,0:T(8,128)(2,1)} %all_to_all.24), calls=%async_computation | async-start | bytes 1048576 | tf_op jit(solution)/shard_map/all_to_all | solution.py:154
  209.4 14.1 %all-to-all-start.1 = ((bf16[16,32,256]{2,1,0:T(8,128)(2,1)}), bf16[16,32,256]{2,1,0:T(8,128)(2,1)S(1)}, u32[]{:S(2)}, u32[]{:S(2)}) async-start(bf16[16,32,256]{2,1,0:T(8,128)(2,1)} %bitcast.44), calls=%async_computation.2 | async-start | bytes 524288 | tf_op jit(solution)/shard_map/all_to_all | solution.py:162
Sparse Core Ops, SparseCore 0:
  9.9 42.6 all-gather.2
  54.3 38.0 all-gather.4
  146.0 61.5 reduce-scatter.1
where the time goes:
time: 233 us; the launch traced here: 232 us
  waiting for transfers between devices  124 us (53%)
  local copies, waits for them, and re-layouts  32.7 us (14%)
  other arithmetic  28.1 us (12%)
  matrix products  18.8 us (8%)
  starting transfers between devices  14.5 us (6%)
  between operations  14.1 us (6%)
    reduce_scatter x1, waiting for transfers between devices, on_device(): lax.psum_scatter(stacked.astype(jnp.bfloat16), 'ctx', scatter_dimension=0...  48.9 us
    all_gather x1, waiting for transfers between devices, on_device(): lax.all_gather(key_mine, 'ctx', axis=0, tiled=True)  36.6 us
    all_gather x1, waiting for transfers between devices, on_device(): lax.all_gather(value_mine, 'ctx', axis=0, tiled=True)  33 us
    all_to_all x1, starting transfers between devices, on_device(): lax.all_to_all(query_local, 'head', split_axis=0, concat_axis=1, tiled=True)  7.25 us
    another operation x5, local copies, waits for them, and re-layouts  7.14 us
    all_to_all x1, starting transfers between devices, on_device(): lax.all_to_all(reduced.astype(jnp.bfloat16), 'head', split_axis=0, concat...  7.09 us
    scatter-add x1, other arithmetic, on_device(): key_acc = jnp.zeros((stretch_total, STRETCH, kv_local, HD), jnp.float32)....  6.12 us
    scatter-add x1, other arithmetic, on_device(): value_acc = jnp.zeros((stretch_total, STRETCH, kv_local, HD), jnp.float32...  6.12 us
  transfers between devices with their start and end apart: 5, of which 4 were waited for; matrix products, arithmetic and copies ran while one was open for 9% of the time, Pallas kernels for 0%

commit v1 on v0

v1 whole, which is shorter than its diff:
```python
import functools

import jax
import jax.numpy as jnp
from jax import lax
from jax.experimental import pallas as pl
from jax.experimental.pallas import tpu as pltpu
from jax.sharding import PartitionSpec as P

HD = 128
STRETCH = 128
REACH = 8
MASKED = -1e30
XROWS = 128
LOG2E = 1.4426950408889634

AG_UPX, AG_UPC, AG_DNC, AG_DNX, AG_YU, AG_YD, AG_SR, AG_SO, AG_N = 0, 4, 7, 11, 14, 18, 21, 29, 37
RS_S, RS_Y, RS_UPX, RS_UPC, RS_DNC, RS_DNX, RS_N = 0, 8, 16, 20, 24, 28, 32


def when(cond, fn):
    if isinstance(cond, bool):
        if cond:
            fn()
    else:
        pl.when(cond)(fn)


def rows(start, size, unit=32):
    return pl.ds(pl.multiple_of(start, unit), size)


def kernel(
    nz, nh,
    order, blocks, q_hbm, k_hbm, v_hbm, g_hbm,
    out_hbm, dq_ref, dk_ref, dv_ref,
    kbuf, vbuf, qcat, gcat, kext, kt, st, wbuf, dst, contrib_v, contrib_k,
    part_v, part_k, sib_v, sib_k, ysend, yrecv, ux, uc, dc, dx, sux, suc, sdc, sdx,
    fin, finrecv, outbuf, dqbuf, dqrecv, slots, bias,
    ag_recv, ag_send, rs_recv, rs_send, fin_recv, fin_send, dq_recv, dq_send, load_sem, out_sem,
):
    ctx = lax.axis_index("ctx")
    head = lax.axis_index("head")
    z, core = ctx // 2, lax.rem(ctx, 2)
    par = lax.rem(head, 2)
    group = head // 2
    local = 4 * STRETCH
    crows = local - 2 * XROWS
    ring_rows = XROWS + crows
    x0, ox0, ring0 = par * 3, 3 - par * 3, par
    far = nz // 2
    short = local // nh
    scale = HD ** (-0.5)

    def zmod(v):
        return lax.rem(v + nz, nz)

    up = {"ctx": zmod(z + 1) * 2 + core}
    down = {"ctx": zmod(z - 1) * 2 + core}
    sib = {"ctx": z * 2 + 1 - core}
    partner = {"head": head + 1 - 2 * par}

    gathered = (kbuf, vbuf)

    def load_kv(t):
        src = (k_hbm, v_hbm)[t].at[:, pl.ds(pl.multiple_of(group * HD, HD), HD)]
        return [
            pltpu.make_async_copy(
                src.at[pl.ds(i * STRETCH, STRETCH)], gathered[t].at[ctx * 4 + i], load_sem.at[t, i]
            )
            for i in range(4)
        ]

    for t in range(2):
        for copy in load_kv(t):
            copy.start()

    def load_qg(n, s, h):
        src, dst_ = ((q_hbm, qcat), (g_hbm, gcat))[n]
        return pltpu.make_async_copy(
            src.at[pl.ds(s * STRETCH, STRETCH), pl.ds(h * HD, HD)],
            dst_.at[s, pl.ds(h * STRETCH, STRETCH)],
            load_sem.at[2 + n, s * 4 + h],
        )

    heads = [(n, s, h) for n in range(2) for s in range(4) for h in range(4)]
    for n, s, h in heads:
        load_qg(n, s, h).start()

    barrier = pltpu.get_barrier_semaphore()
    for who in (up, down, sib):
        pl.semaphore_signal(barrier, inc=1, device_id=who, device_id_type=pl.DeviceIdType.MESH)
    for i in range(1, nh):
        pl.semaphore_signal(
            barrier, inc=1, device_id={"head": lax.rem(head + i, nh)},
            device_id_type=pl.DeviceIdType.MESH,
        )

    zero_row = jnp.zeros((STRETCH, HD), jnp.float32)
    contrib_v[4 * REACH] = zero_row
    contrib_k[4 * REACH] = zero_row
    for t in range(2):
        ux[t, 0] = jnp.zeros((XROWS, HD), jnp.bfloat16)
        dc[t, 0] = jnp.zeros((2, STRETCH, HD), jnp.bfloat16)
        uc[t, 1] = jnp.zeros((2, STRETCH, HD), jnp.bfloat16)
        dx[t, 1] = jnp.zeros((XROWS, HD), jnp.bfloat16)
    first_b = XROWS // short
    last_b = (local - XROWS) // short

    def fill(p):
        for t in range(2):
            for i in range(nh // 2):
                finrecv[t, 2 * i + p] = jnp.zeros((short, HD), jnp.bfloat16)

    pl.when(head >= last_b)(lambda: fill(0))
    pl.when(head < first_b)(lambda: fill(1))

    pl.semaphore_wait(barrier, nh + 2)

    def piece(t, z_of, core_of, start, size):
        return gathered[t].at[pl.ds((z_of * 2 + core_of) * 4 + start, size)]

    def ag_copy(t, z_of, start, size, sem, device):
        ref = piece(t, z_of, core, start, size)
        return pltpu.make_async_remote_copy(
            src_ref=ref, dst_ref=ref, send_sem=ag_send.at[t, sem], recv_sem=ag_recv.at[t, sem],
            device_id=device, device_id_type=pl.DeviceIdType.MESH,
        )

    def ag_wait(t, z_of, core_of, start, size, sem):
        ref = piece(t, z_of, core_of, start, size)
        pltpu.make_async_remote_copy(
            src_ref=ref, dst_ref=ref, send_sem=ag_send.at[t, sem], recv_sem=ag_recv.at[t, sem],
            device_id=up, device_id_type=pl.DeviceIdType.MESH,
        ).wait_recv()

    def ag_first(t):
        for copy in load_kv(t):
            copy.wait()
        ag_copy(t, z, x0, 1, AG_UPX, up).start()
        ag_copy(t, z, 1, 2, AG_DNC, down).start()
        ag_copy(t, z, 1, 2, AG_UPC, up).start()
        ag_copy(t, z, x0, 1, AG_DNX, down).start()
        ag_copy(t, z, ring0, 3, AG_SR, sib).start()
        ag_copy(t, z, ox0, 1, AG_SO, sib).start()

    def ag_partner(t, k):
        zo = zmod(z - k)
        ag_wait(t, zo, core, ox0, 1, AG_YU + k - 1)
        ag_copy(t, zo, ox0, 1, AG_SO + k, sib).start()

        def lower():
            zd = zmod(z + k)
            ag_wait(t, zd, core, ox0, 1, AG_YD + k - 1)
            ag_copy(t, zd, ox0, 1, AG_SO + nz - k, sib).start()

        when(k < far, lower)

    def ag_step(t, k):
        zo, zd = zmod(z - k), zmod(z + k)
        ag_wait(t, zo, core, x0, 1, AG_UPX + k - 1)
        when(k < far, lambda: ag_copy(t, zo, x0, 1, AG_UPX + k, up).start())
        ag_copy(t, zo, x0, 1, AG_YU + k - 1, partner).start()
        ag_wait(t, zd, core, 1, 2, AG_DNC + k - 1)
        when(k < far, lambda: ag_copy(t, zd, 1, 2, AG_DNC + k, down).start())

        def near():
            ag_wait(t, zo, core, 1, 2, AG_UPC + k - 1)
            when(k < far - 1, lambda: ag_copy(t, zo, 1, 2, AG_UPC + k, up).start())
            ag_wait(t, zd, core, x0, 1, AG_DNX + k - 1)
            when(k < far - 1, lambda: ag_copy(t, zd, x0, 1, AG_DNX + k, down).start())
            ag_copy(t, zd, x0, 1, AG_YD + k - 1, partner).start()
            ag_copy(t, zd, ring0, 3, AG_SR + nz - k, sib).start()

        when(k < far, near)
        ag_copy(t, zo, ring0, 3, AG_SR + k, sib).start()
        when(k > 1, lambda: ag_partner(t, k - 1))

    def ag_finish(t):
        ag_partner(t, far)

        @pl.loop(0, nz)
        def _(d):
            zo = zmod(z - d)
            ag_wait(t, zo, 1 - core, ring0, 3, AG_SR + d)
            ag_wait(t, zo, 1 - core, ox0, 1, AG_SO + d)

    def tables():
        total = order.shape[0]
        for s in range(4):
            own = order[ctx * 4 + s]

            def seek(i, found):
                here = order[i]
                return tuple(
                    jnp.where(here == own - (REACH - 1) + j, i, found[j]) for j in range(REACH)
                )

            found = lax.fori_loop(0, total, seek, (jnp.int32(0),) * REACH)

            def begin(i, carry):
                end, start = carry
                end = end + blocks[i]
                return end, jnp.where(end <= own, end, start)

            _, start = lax.fori_loop(
                0, blocks.shape[0], begin, (jnp.int32(0), jnp.int32(0))
            )
            for j in range(REACH):
                slots[s * REACH + j] = found[j]
                bias[s * REACH + j] = jnp.where(
                    own - (REACH - 1) + j >= start, jnp.float32(0.0), jnp.float32(MASKED)
                )

    nt = (((1,), (1,)), ((), ()))
    nn = (((1,), (0,)), ((), ()))

    def dot(a, b, dims):
        return lax.dot_general(a, b, dims, preferred_element_type=jnp.float32)

    def block(j):
        return pl.ds(pl.multiple_of(j * STRETCH, STRETCH), STRETCH)

    def extent(t, s):
        for j in range(REACH):
            value = gathered[t][slots[s * REACH + j]]
            kext[pl.ds(j * STRETCH, STRETCH), :] = value
            kt[:, pl.ds(j * STRETCH, STRETCH)] = value.T

    def fold(value, op):
        return op(value.reshape(STRETCH // 8, 8, value.shape[1]), axis=0)

    def forward(s):
        q = qcat[s]
        for j in range(REACH):
            kext[pl.ds(j * STRETCH, STRETCH), :] = kbuf[slots[s * REACH + j]]
        st[...] = dot(kext[...], q, nt)
        key_at = lax.broadcasted_iota(jnp.int32, (STRETCH, STRETCH), 0)
        query_at = lax.broadcasted_iota(jnp.int32, (STRETCH, STRETCH), 1)
        causal = key_at <= query_at
        diag = pl.ds((REACH - 1) * STRETCH, STRETCH)
        raw = st[diag, :] * (scale * LOG2E)
        raw = jnp.concatenate(
            [jnp.where(causal, raw[:, h * HD:(h + 1) * HD], MASKED) for h in range(4)], axis=1
        )
        st[diag, :] = raw

        def highest(j, top):
            value = st[block(j), :] * (scale * LOG2E) + bias[s * REACH + j]
            st[block(j), :] = value
            return jnp.maximum(top, fold(value, jnp.max))

        top = lax.fori_loop(0, REACH - 1, highest, fold(raw, jnp.max))
        top = jnp.max(top, axis=0, keepdims=True)

        def exps(j, total):
            value = jnp.exp2(st[block(j), :] - top)
            st[block(j), :] = value
            return total + fold(value, jnp.sum)

        total = lax.fori_loop(0, REACH, exps, jnp.zeros((8, 512), jnp.float32))
        inverse = 1.0 / jnp.sum(total, axis=0, keepdims=True)

        @pl.loop(0, REACH)
        def _(j):
            wbuf[s, block(j), :] = (
                st[block(j), :] * inverse
            ).astype(jnp.bfloat16)

        contrib_v[pl.ds(s * REACH, REACH)] = dot(
            wbuf[s], gcat[s], nn
        ).reshape(REACH, STRETCH, HD)

    per = STRETCH // short

    def backward(s):
        g = gcat[s]
        extent(1, s)
        st[...] = dot(kext[...], g, nt)
        ot = dot(kt[...], wbuf[s], nn).astype(jnp.bfloat16)
        ot = ot.astype(jnp.float32)
        dots = []
        for h in range(4):
            part = ot[:, h * HD:(h + 1) * HD]
            outbuf[s, :, pl.ds(h * HD, HD)] = part.T.astype(jnp.bfloat16)
            gt = g[h * STRETCH:(h + 1) * STRETCH, :].astype(jnp.float32).T
            dots.append(jnp.sum(gt * part, axis=0, keepdims=True))
        dots = jnp.concatenate(dots, axis=1)
        pltpu.make_async_copy(
            outbuf.at[s],
            out_hbm.at[rows(s * STRETCH, STRETCH, STRETCH)], out_sem.at[s],
        ).start()

        @pl.loop(0, REACH)
        def _(j):
            w = wbuf[s, block(j), :].astype(jnp.float32)
            dst[block(j), :] = (w * (st[block(j), :] - dots)).astype(jnp.bfloat16)

        contrib_k[pl.ds(s * REACH, REACH)] = (
            dot(dst[...], qcat[s], nn) * scale
        ).reshape(REACH, STRETCH, HD)
        extent(0, s)
        dqt = dot(kt[...], dst[...], nn) * scale
        for h in range(4):
            dqbuf[pl.ds(s * per, per), :, pl.ds(h * HD, HD)] = dqt[
                :, h * HD:(h + 1) * HD
            ].T.reshape(per, short, HD).astype(jnp.bfloat16)

        @pl.loop(0, per)
        def _(i):
            b = s * per + i

            def remote():
                dq_copy(b, head, b).start()

            def own():
                dqrecv[head] = dqbuf[b]

            pl.when(b != head)(remote)
            pl.when(b == head)(own)

    def dq_copy(b, src, to):
        return pltpu.make_async_remote_copy(
            src_ref=dqbuf.at[b], dst_ref=dqrecv.at[src],
            send_sem=dq_send.at[b], recv_sem=dq_recv.at[src],
            device_id={"head": to}, device_id_type=pl.DeviceIdType.MESH,
        )

    contribs = (contrib_k, contrib_v)
    parts = (part_k, part_v)
    sibs = (sib_k, sib_v)

    def build(t, at):
        for k in range(4):
            here = order[at * 4 + k]
            total = None
            for s in range(4):
                delta = order[ctx * 4 + s] - here
                index = jnp.where(
                    (delta >= 0) & (delta < REACH), s * REACH + REACH - 1 - delta, 4 * REACH
                )
                term = contribs[t][index]
                total = term if total is None else total + term
            parts[t][at * 4 + k] = total.astype(jnp.bfloat16)

    def rs_copy(t, src, dst_, sem, device):
        return pltpu.make_async_remote_copy(
            src_ref=src, dst_ref=dst_, send_sem=rs_send.at[t, sem], recv_sem=rs_recv.at[t, sem],
            device_id=device, device_id_type=pl.DeviceIdType.MESH,
        )

    def rs_wait(t, ref, sem):
        rs_copy(t, ref, ref, sem, up).wait_recv()

    def dest(i):
        return zmod(z + far + ((i + 1) // 2) * (2 * lax.rem(i, 2) - 1))

    def rs_build(t):
        @pl.loop(0, nz)
        def _(i):
            zt = dest(i)
            other = zt * 2 + 1 - core
            build(t, other)
            rs_copy(
                t, parts[t].at[pl.ds(other * 4, 4)], sibs[t].at[pl.ds(i * 4, 4)], RS_S + i, sib
            ).start()
            build(t, zt * 2 + core)

    def place(i):
        if i == nz - 1:
            return z
        delta = far + ((i + 1) // 2) * (2 * (i % 2) - 1)
        return zmod(z + delta)

    def chip_sum(t, i, start, size):
        return (
            parts[t][pl.ds((place(i) * 2 + core) * 4 + start, size)].astype(jnp.float32)
            + sibs[t][pl.ds(i * 4 + start, size)].astype(jnp.float32)
        )

    def rs_partner(t):
        for i in range(nz):
            rs_wait(t, sibs[t].at[pl.ds(i * 4, 4)], RS_S + i)
            ysend[t, i] = chip_sum(t, i, ox0, 1)[0].astype(jnp.bfloat16)
            rs_copy(t, ysend.at[t, i], yrecv.at[t, i], RS_Y + i, partner).start()

    def own_x(t, i):
        rs_wait(t, yrecv.at[t, i], RS_Y + i)
        return chip_sum(t, i, x0, 1)[0] + yrecv[t, i].astype(jnp.float32)

    def own_c(t, i):
        return chip_sum(t, i, 1, 2)

    def rs_step(t, k):
        iu, idn = 2 * (k - 1), max(0, 2 * k - 3)
        when(k > 1, lambda: rs_wait(t, ux.at[t, k - 1], RS_UPX + k - 2))
        sux[t, k] = (own_x(t, iu) + ux[t, k - 1].astype(jnp.float32)).astype(jnp.bfloat16)
        rs_copy(t, sux.at[t, k], ux.at[t, k], RS_UPX + k - 1, up).start()
        when(k > 1, lambda: rs_wait(t, dc.at[t, k - 1], RS_DNC + k - 2))
        sdc[t, k] = (own_c(t, idn) + dc[t, k - 1].astype(jnp.float32)).astype(jnp.bfloat16)
        rs_copy(t, sdc.at[t, k], dc.at[t, k], RS_DNC + k - 1, down).start()

        def near():
            when(k > 2, lambda: rs_wait(t, uc.at[t, k - 1], RS_UPC + k - 2))
            suc[t, k] = (own_c(t, iu) + uc[t, k - 1].astype(jnp.float32)).astype(jnp.bfloat16)
            rs_copy(t, suc.at[t, k], uc.at[t, k], RS_UPC + k - 1, up).start()
            when(k > 2, lambda: rs_wait(t, dx.at[t, k - 1], RS_DNX + k - 2))
            sdx[t, k] = (own_x(t, idn) + dx[t, k - 1].astype(jnp.float32)).astype(jnp.bfloat16)
            rs_copy(t, sdx.at[t, k], dx.at[t, k], RS_DNX + k - 1, down).start()

        when(k > 1, near)

    b0 = par * (XROWS // short)
    nb = ring_rows // short
    own_in = (head >= b0) & (head < b0 + nb)

    def fin_copy(t, b, src):
        return pltpu.make_async_remote_copy(
            src_ref=fin.at[t, rows(b * short, short)], dst_ref=finrecv.at[t, src],
            send_sem=fin_send.at[t, b], recv_sem=fin_recv.at[t, src],
            device_id={"head": b}, device_id_type=pl.DeviceIdType.MESH,
        )

    def rs_final(t):
        rs_wait(t, ux.at[t, far], RS_UPX + far - 1)
        rs_wait(t, dx.at[t, far], RS_DNX + far - 1)
        fin[t, rows(x0 * STRETCH, XROWS), :] = (
            own_x(t, nz - 1) + ux[t, far].astype(jnp.float32) + dx[t, far].astype(jnp.float32)
        ).astype(jnp.bfloat16)
        rs_wait(t, uc.at[t, far], RS_UPC + far - 1)
        rs_wait(t, dc.at[t, far], RS_DNC + far - 1)
        fin[t, pl.ds(XROWS, crows), :] = (
            own_c(t, nz - 1) + uc[t, far].astype(jnp.float32) + dc[t, far].astype(jnp.float32)
        ).reshape(crows, HD).astype(jnp.bfloat16)

        @pl.loop(0, nb)
        def _(i):
            b = b0 + i
            pl.when(b != head)(lambda: fin_copy(t, b, head).start())

            def keep():
                finrecv[t, head] = fin[t, rows(head * short, short), :]

            pl.when(b == head)(keep)

    def rs_out(t, ref):
        @pl.loop(0, nh)
        def _(src):
            p = lax.rem(src, 2)
            sends = ((p == 0) & (head < last_b)) | ((p == 1) & (head >= first_b))
            pl.when(sends & (src != head))(lambda: fin_copy(t, 0, src).wait_recv())

        for g in range(nh // 2):
            ref[:, g * HD:(g + 1) * HD] = (
                finrecv[t, 2 * g].astype(jnp.float32) + finrecv[t, 2 * g + 1].astype(jnp.float32)
            ).astype(jnp.bfloat16)

    ag_first(0)
    tables()

    @pl.loop(1, far)
    def _(k):
        ag_step(0, k)

    ag_first(1)
    ag_step(0, far)
    ag_finish(0)
    for n, s, h in heads:
        load_qg(n, s, h).wait()
    ag_step(1, 1)

    @pl.loop(0, 4)
    def _(s):
        forward(s)
        pl.when(s < far - 1)(lambda: ag_step(1, s + 2))

    ag_finish(1)
    rs_build(1)
    rs_partner(1)
    rs_step(1, 1)

    for s in range(4):
        backward(s)
        if s < far - 1:
            rs_step(1, s + 2)

    rs_build(0)
    rs_partner(0)
    rs_step(0, 1)
    rs_final(1)

    for k in range(2, far + 1):
        rs_step(0, k)

    rs_out(1, dv_ref)
    rs_final(0)
    rs_out(0, dk_ref)

    @pl.loop(0, nh)
    def _(src):
        pl.when(src != head)(lambda: dq_copy(0, src, src).wait_recv())

    for src in range(nh):
        dq_ref[:, src * 4 * HD:(src + 1) * 4 * HD] = dqrecv[src]
    @pl.loop(0, nh)
    def _(b):
        pl.when(b != head)(lambda: dq_copy(b, head, b).wait_send())

    for s in range(4):
        pltpu.make_async_copy(
            outbuf.at[s], out_hbm.at[pl.ds(s * STRETCH, STRETCH)], out_sem.at[s]
        ).wait()
    for t in range(2):
        for first, count, size in (
            (AG_UPX, far, 1), (AG_UPC, far - 1, 2), (AG_DNC, far, 2), (AG_DNX, far - 1, 1),
            (AG_YU, far, 1), (AG_YD, far - 1, 1), (AG_SR, nz, 3), (AG_SO, nz, 1),
        ):

            @pl.loop(first, first + count)
            def _(sem):
                ag_copy(t, z, 0, size, sem, up).wait_send()

        for first, count, ref in (
            (RS_S, nz, sibs[t].at[pl.ds(0, 4)]), (RS_Y, nz, yrecv.at[t, 0]),
            (RS_UPX, far, ux.at[t, 0]), (RS_UPC + 1, far - 1, uc.at[t, 0]),
            (RS_DNC, far, dc.at[t, 0]), (RS_DNX + 1, far - 1, dx.at[t, 0]),
        ):

            @pl.loop(first, first + count)
            def _(sem):
                rs_copy(t, ref, ref, sem, up).wait_send()

        @pl.loop(0, nb)
        def _(i):
            pl.when(b0 + i != head)(lambda: fin_copy(t, b0 + i, head).wait_send())


def on_device(query_states, key_states, value_states, out_grad, stretch_order, doc_blocks):
    nz = lax.axis_size("ctx") // 2
    nh = lax.axis_size("head")
    far = nz // 2
    local = 4 * STRETCH
    crows = local - 2 * XROWS
    short = local // nh
    seq = 2 * nz * local
    bf, f32 = jnp.bfloat16, jnp.float32
    anywhere = pl.BlockSpec(memory_space=pl.ANY)
    smem = pl.BlockSpec(memory_space=pltpu.SMEM)
    vmem = pl.BlockSpec(memory_space=pltpu.VMEM)
    V, D = pltpu.VMEM, pltpu.SemaphoreType.DMA
    return pl.pallas_call(
        functools.partial(kernel, nz, nh),
        out_shape=(
            jax.ShapeDtypeStruct((local, 4 * HD), bf),
            jax.ShapeDtypeStruct((short, nh * 4 * HD), bf),
            jax.ShapeDtypeStruct((short, nh // 2 * HD), bf),
            jax.ShapeDtypeStruct((short, nh // 2 * HD), bf),
        ),
        in_specs=[smem, smem, anywhere, anywhere, anywhere, anywhere],
        out_specs=(anywhere, vmem, vmem, vmem),
        scratch_shapes=[
            V((seq // STRETCH, STRETCH, HD), bf), V((seq // STRETCH, STRETCH, HD), bf),
            V((4, 512, HD), bf), V((4, 512, HD), bf),
            V((1024, HD), bf), V((HD, 1024), bf),
            V((1024, 512), f32), V((4, 1024, 512), bf), V((1024, 512), bf),
            V((4 * REACH + 1, STRETCH, HD), f32), V((4 * REACH + 1, STRETCH, HD), f32),
            V((seq // STRETCH, STRETCH, HD), bf), V((seq // STRETCH, STRETCH, HD), bf),
            V((nz * 4, STRETCH, HD), bf), V((nz * 4, STRETCH, HD), bf),
            V((2, nz, XROWS, HD), bf), V((2, nz, XROWS, HD), bf),
            V((2, far + 1, XROWS, HD), bf), V((2, far + 1, 2, STRETCH, HD), bf),
            V((2, far + 1, 2, STRETCH, HD), bf), V((2, far + 1, XROWS, HD), bf),
            V((2, far + 1, XROWS, HD), bf), V((2, far + 1, 2, STRETCH, HD), bf),
            V((2, far + 1, 2, STRETCH, HD), bf), V((2, far + 1, XROWS, HD), bf),
            V((2, local, HD), bf), V((2, nh, short, HD), bf),
            V((4, STRETCH, 4 * HD), bf), V((nh, short, 4 * HD), bf), V((nh, short, 4 * HD), bf),
            pltpu.SMEM((4 * REACH,), jnp.int32), pltpu.SMEM((4 * REACH,), f32),
            D((2, AG_N)), D((2, AG_N)), D((2, RS_N)), D((2, RS_N)),
            D((2, nh)), D((2, nh)), D((nh,)), D((nh,)), D((4, 16)), D((4,)),
        ],
        compiler_params=pltpu.CompilerParams(
            collective_id=0, has_side_effects=True, vmem_limit_bytes=56 * 1024 * 1024
        ),
        cost_estimate=pl.CostEstimate(
            flops=3_300_000_000, bytes_accessed=4_000_000, transcendentals=2_100_000
        ),
    )(stretch_order, doc_blocks, query_states, key_states, value_states, out_grad)


def solution(mesh):
    in_specs = (P("ctx", "head"), P("ctx", None), P("ctx", None), P("ctx", "head"), P(), P())
    out_specs = (
        P("ctx", "head"),
        P(("ctx", "head"), None),
        P(("ctx", "head"), None),
        P(("ctx", "head"), None),
    )
    return jax.shard_map(
        on_device, mesh=mesh, in_specs=in_specs, out_specs=out_specs, check_vma=False
    )
```

time: 233 us -> 95.9 us (0.41)
  waiting for transfers between devices: 124 us -> 0 us
  Pallas kernels: 0 us -> 90.8 us
  local copies, waits for them, and re-layouts: 32.7 us -> 4.28 us
  other arithmetic: 28.1 us -> 0 us
  matrix products: 18.8 us -> 0 us
  starting transfers between devices: 14.5 us -> 0 us
  between operations: 14.1 us -> 0.65 us
    pallas_call x0 -> x1, Pallas kernels: none -> 90.8 us  [on_device(): pl.pallas_call(functools.partial(kernel, nz, nh), out_shape=(jax.ShapeDty...]
    all_gather x2 -> x0, waiting for transfers between devices: 69.7 us -> none  [the longest x1 36.6 us: on_device(): lax.all_gather(key_mine, 'ctx', axis=0, tiled=True)]
    reduce_scatter x1 -> x0, waiting for transfers between devices: 48.9 us -> none  [on_device(): lax.psum_scatter(stacked.astype(jnp.bfloat16), 'ctx', scatter_dimension=0...]
    dot_general x6 -> x0, matrix products: 18.8 us -> none  [the longest x1 4.3 us: attend(): jnp.einsum('cqgjd,ckgd->cgjqk', grad_block, value_block, preferred_elemen...]
    all_to_all x2 -> x0, starting transfers between devices: 14.3 us -> none  [the longest x1 7.25 us: on_device(): lax.all_to_all(query_local, 'head', split_axis=0, concat_axis=1, tiled=True)]
    scatter-add x2 -> x0, other arithmetic: 12.2 us -> none  [the longest x1 6.12 us: on_device(): key_acc = jnp.zeros((stretch_total, STRETCH, kv_local, HD), jnp.float32)....]
    another operation x6 -> x0, local copies, waits for them, and re-layouts: 10.1 us -> none
    another operation x4 -> x0, other arithmetic: 9.97 us -> none
  transfers between devices with their start and end apart: 5 -> 0, of which waited for: 4 -> 0; matrix products, arithmetic and copies ran while one was open for 9% -> 0% of each run, Pallas kernels for 0% -> 0%
where the time goes in v1:
time: 95.9 us; the launch traced here: 95.7 us
  Pallas kernels  90.8 us (95%)
  local copies, waits for them, and re-layouts  4.28 us (4%)
    pallas_call x1, Pallas kernels, on_device(): pl.pallas_call(functools.partial(kernel, nz, nh), out_shape=(jax.ShapeDty...  90.8 us
    unnamed x10, local copies, waits for them, and re-layouts  4.28 us

profile of v1, /device:TPU:8, one launch (start us, length us, event | category | flops | bytes accessed | tf_op | source)
XLA Modules:
  0.0 95.7 jit_solution(12205917844677736949)
XLA Ops:
  0.6 90.8 %shard_map.93 = (bf16[512,512]{1,0:T(8,128)(2,1)}, bf16[32,8192]{1,0:T(8,128)(2,1)}, bf16[32,1024]{1,0:T(8,128)(2,1)}, bf16[32,1024]{1,0:T(8,128)(2,1)}) custom-call(s32[64]{0:T(128)} %order.1, s32[16]{0:T(128)} %blocks.1, bf16[512,512]{1,0:T(8,128)(2,1)} %q_hbm.1, bf16[512,1024]{1,0:T(8,128)(2,1)} %k_hbm.1, bf16[512,1024]{1,0:T(8,128)(2,1)} %v_hbm.1, ...), custom_call_target="tpu_custom_call" | custom-call | flops 3300000000 | bytes 4000000 | tf_op jit(solution)/shard_map/pallas_call | solution.py:551
  91.4 0.0 copy-start
  91.4 1.9 %copy.14 = bf16[512,512]{1,0:T(8,128)(2,1)} copy(bf16[512,512]{1,0:T(8,128)(2,1)} %get-tuple-element.8) | data formatting | bytes 1048576
  93.3 0.0 copy-done
  93.3 0.0 copy-start.2
  93.4 0.8 copy.15
  94.1 0.1 copy-done.2
  94.2 0.0 copy-start.1
  94.2 0.6 copy.16
  94.8 0.2 copy-done.1
  95.1 0.6 copy.17
Async XLA Ops:
  91.4 1.9 %copy-start = (bf16[32,8192]{1,0:T(8,128)(2,1)S(1)}, bf16[32,8192]{1,0:T(8,128)(2,1)}, u32[]{:S(2)}) copy-start(bf16[32,8192]{1,0:T(8,128)(2,1)} %get-tuple-element.9) | copy-start | bytes 1572868
  93.3 0.9 copy-start.2
  94.2 0.9 copy-start.1

commit v2 on v1

v2 whole, which is shorter than its diff:
```python
import functools

import jax
import jax.numpy as jnp
from jax import lax
from jax.experimental import pallas as pl
from jax.experimental.pallas import tpu as pltpu
from jax.sharding import PartitionSpec as P

HD = 128
STRETCH = 128
REACH = 8
MASKED = -1e30
XROWS = 128
LOG2E = 1.4426950408889634

AG_Y, AG_SR, AG_SO, AG_N = 24, 32, 40, 48
RS_S, RS_Y, RS_N = 24, 32, 40
UP, DOWN = 0, 1
ORDER = ((UP, 0), (DOWN, 1), (UP, 1), (DOWN, 2), (UP, 2), (DOWN, 0))


def when(cond, fn):
    if isinstance(cond, bool):
        if cond:
            fn()
    else:
        pl.when(cond)(fn)


def rows(start, size, unit=32):
    return pl.ds(pl.multiple_of(start, unit), size)


def kernel(
    nz, nh,
    order, blocks, q_hbm, k_hbm, v_hbm, g_hbm,
    out_hbm, dq_ref, dk_ref, dv_ref,
    kbuf, vbuf, qcat, gcat, kext, kt, st, wbuf, row_top, contrib_v, contrib_k,
    part_v, part_k, sib_v, sib_k, ysend, yrecv, ring_in, ring_out,
    fin, finrecv, outbuf, dqbuf, dqrecv, slots, bias,
    ag_recv, ag_send, rs_recv, rs_send, fin_recv, fin_send, dq_recv, dq_send, load_sem, out_sem,
):
    ctx = lax.axis_index("ctx")
    head = lax.axis_index("head")
    z, core = ctx // 2, lax.rem(ctx, 2)
    par = lax.rem(head, 2)
    group = head // 2
    local = 4 * STRETCH
    crows = local - 2 * XROWS
    ring_rows = XROWS + crows
    x0, ox0, ring0 = par * 3, 3 - par * 3, par
    far = nz // 2
    short = local // nh
    scale = HD ** (-0.5)

    def zmod(v):
        return lax.rem(v + nz, nz)

    up = {"ctx": zmod(z + 1) * 2 + core}
    down = {"ctx": zmod(z - 1) * 2 + core}
    sib = {"ctx": z * 2 + 1 - core}
    partner = {"head": head + 1 - 2 * par}

    gathered = (kbuf, vbuf)

    def load_kv(t):
        src = (k_hbm, v_hbm)[t].at[:, pl.ds(pl.multiple_of(group * HD, HD), HD)]
        return [
            pltpu.make_async_copy(
                src.at[pl.ds(i * STRETCH, STRETCH)], gathered[t].at[ctx * 4 + i], load_sem.at[t, i]
            )
            for i in range(4)
        ]

    for t in range(2):
        for copy in load_kv(t):
            copy.start()

    def load_qg(n, s, h):
        src, dst_ = ((q_hbm, qcat), (g_hbm, gcat))[n]
        return pltpu.make_async_copy(
            src.at[pl.ds(s * STRETCH, STRETCH), pl.ds(h * HD, HD)],
            dst_.at[s, pl.ds(h * STRETCH, STRETCH)],
            load_sem.at[2 + n, s * 4 + h],
        )

    heads = [(n, s, h) for n in range(2) for s in range(4) for h in range(4)]
    for n, s, h in heads:
        load_qg(n, s, h).start()

    barrier = pltpu.get_barrier_semaphore()
    for who in (up, down, sib):
        pl.semaphore_signal(barrier, inc=1, device_id=who, device_id_type=pl.DeviceIdType.MESH)
    for i in range(1, nh):
        pl.semaphore_signal(
            barrier, inc=1, device_id={"head": lax.rem(head + i, nh)},
            device_id_type=pl.DeviceIdType.MESH,
        )

    zero_row = jnp.zeros((STRETCH, HD), jnp.float32)
    contrib_v[4 * REACH] = zero_row
    contrib_k[4 * REACH] = zero_row
    first_b = XROWS // short
    last_b = (local - XROWS) // short

    def fill(p):
        for t in range(2):
            for i in range(nh // 2):
                finrecv[t, 2 * i + p] = jnp.zeros((short, HD), jnp.bfloat16)

    pl.when(head >= last_b)(lambda: fill(0))
    pl.when(head < first_b)(lambda: fill(1))

    def tables():
        total = order.shape[0]
        for s in range(4):
            own = order[ctx * 4 + s]

            def seek(i, found):
                here = order[i]
                return tuple(
                    jnp.where(here == own - (REACH - 1) + j, i, found[j]) for j in range(REACH)
                )

            found = lax.fori_loop(0, total, seek, (jnp.int32(0),) * REACH)

            def begin(i, carry):
                end, start = carry
                end = end + blocks[i]
                return end, jnp.where(end <= own, end, start)

            _, start = lax.fori_loop(
                0, blocks.shape[0], begin, (jnp.int32(0), jnp.int32(0))
            )
            for j in range(REACH):
                slots[s * REACH + j] = found[j]
                bias[s * REACH + j] = jnp.where(
                    own - (REACH - 1) + j >= start, jnp.float32(0.0), jnp.float32(MASKED)
                )

    tables()
    pl.semaphore_wait(barrier, nh + 2)

    def piece(t, z_of, core_of, start, size):
        return gathered[t].at[pl.ds((z_of * 2 + core_of) * 4 + start, size)]

    def ag_copy(t, z_of, start, size, sem, device):
        ref = piece(t, z_of, core, start, size)
        return pltpu.make_async_remote_copy(
            src_ref=ref, dst_ref=ref, send_sem=ag_send.at[t, sem], recv_sem=ag_recv.at[t, sem],
            device_id=device, device_id_type=pl.DeviceIdType.MESH,
        )

    def ag_wait(t, z_of, core_of, start, size, sem):
        ref = piece(t, z_of, core_of, start, size)
        pltpu.make_async_remote_copy(
            src_ref=ref, dst_ref=ref, send_sem=ag_send.at[t, sem], recv_sem=ag_recv.at[t, sem],
            device_id=up, device_id_type=pl.DeviceIdType.MESH,
        ).wait_recv()

    def at_unit(u):
        return x0 if u == 0 else u

    def chain(way, u):
        return (way * 3 + u) * 4

    def hops(way, u):
        return far if (way == UP) == (u == 0) else far - 1

    def ag_first(t):
        for copy in load_kv(t):
            copy.wait()
        for way, u in ORDER:
            ag_copy(t, z, at_unit(u), 1, chain(way, u), (up, down)[way]).start()
        ag_copy(t, z, ring0, 3, AG_SR, sib).start()
        ag_copy(t, z, ox0, 1, AG_SO, sib).start()

    def ag_partner(t, k):
        zo = zmod(z - k)
        ag_wait(t, zo, core, ox0, 1, AG_Y + k - 1)
        ag_copy(t, zo, ox0, 1, AG_SO + k, sib).start()

        def lower():
            zd = zmod(z + k)
            ag_wait(t, zd, core, ox0, 1, AG_Y + 3 + k)
            ag_copy(t, zd, ox0, 1, AG_SO + nz - k, sib).start()

        when(k < far, lower)

    def ag_step(t, k):
        ag_half(t, k, 0)
        ag_half(t, k, 1)

    def ag_half(t, k, half):
        zo, zd = zmod(z - k), zmod(z + k)
        for way, u in ORDER[3 * half:3 * half + 3]:
            origin, sem, last = (zo, zd)[way], chain(way, u), hops(way, u)

            def pass_on(way=way, u=u, origin=origin, sem=sem, last=last):
                ag_wait(t, origin, core, at_unit(u), 1, sem + k - 1)

                def send():
                    ag_copy(t, origin, at_unit(u), 1, sem + k, (up, down)[way]).start()

                when(k < last, send)
                if u == 0:
                    ag_copy(t, origin, x0, 1, AG_Y + 4 * way + k - 1, partner).start()

            when(k <= last, pass_on)
        if half == 1:
            ag_copy(t, zo, ring0, 3, AG_SR + k, sib).start()
            when(k < far, lambda: ag_copy(t, zd, ring0, 3, AG_SR + nz - k, sib).start())
            when(k > 1, lambda: ag_partner(t, k - 1))

    def ag_finish(t):
        ag_partner(t, far)

        @pl.loop(0, nz)
        def _(d):
            zo = zmod(z - d)
            ag_wait(t, zo, 1 - core, ring0, 3, AG_SR + d)
            ag_wait(t, zo, 1 - core, ox0, 1, AG_SO + d)

    nt = (((1,), (1,)), ((), ()))
    nn = (((1,), (0,)), ((), ()))

    def dot(a, b, dims):
        return lax.dot_general(a, b, dims, preferred_element_type=jnp.float32)

    def fold(value, op):
        return op(value.reshape(STRETCH // 8, 8, value.shape[1]), axis=0)

    def scores(s):
        for j in range(REACH):
            kext[pl.ds(j * STRETCH, STRETCH), :] = kbuf[slots[s * REACH + j]]
        st[...] = dot(kext[...], qcat[s], nt)
        key_at = lax.broadcasted_iota(jnp.int32, (STRETCH, STRETCH), 0)
        query_at = lax.broadcasted_iota(jnp.int32, (STRETCH, STRETCH), 1)
        causal = key_at <= query_at
        diag = pl.ds((REACH - 1) * STRETCH, STRETCH)
        raw = st[diag, :]
        raw = jnp.concatenate(
            [jnp.where(causal, raw[:, h * HD:(h + 1) * HD], MASKED) for h in range(4)], axis=1
        )
        st[diag, :] = raw

        top = fold(raw, jnp.max)
        for j in range(REACH - 1):
            high = fold(st[pl.ds(j * STRETCH, STRETCH), :], jnp.max)
            top = jnp.maximum(top, high + bias[s * REACH + j])
        row_top[...] = jnp.max(top, axis=0, keepdims=True)

    def softmax(s):
        top = row_top[...]
        total = jnp.zeros((8, 512), jnp.float32)
        for j in range(REACH):
            shift = bias[s * REACH + j] - top
            at = pl.ds(j * STRETCH, STRETCH)
            value = jnp.exp2((st[at, :] + shift) * (scale * LOG2E))
            st[at, :] = value
            total = total + fold(value, jnp.sum)
        inverse = 1.0 / jnp.sum(total, axis=0, keepdims=True)
        for j in range(REACH):
            at = pl.ds(j * STRETCH, STRETCH)
            wbuf[s, at, :] = (st[at, :] * inverse).astype(jnp.bfloat16)
        contrib_v[pl.ds(s * REACH, REACH)] = dot(wbuf[s], gcat[s], nn).reshape(REACH, STRETCH, HD)

    per = STRETCH // short

    def key_side(s):
        g = gcat[s]
        for j in range(REACH):
            value = vbuf[slots[s * REACH + j]]
            kext[pl.ds(j * STRETCH, STRETCH), :] = value
            kt[:, pl.ds(j * STRETCH, STRETCH)] = value.T
        st[...] = dot(kext[...], g, nt)
        ot = dot(kt[...], wbuf[s], nn).astype(jnp.bfloat16)
        ot = ot.astype(jnp.float32)
        dots = []
        for h in range(4):
            part = ot[:, h * HD:(h + 1) * HD]
            outbuf[s, :, pl.ds(h * HD, HD)] = part.T.astype(jnp.bfloat16)
            gt = g[h * STRETCH:(h + 1) * STRETCH, :].astype(jnp.float32).T
            dots.append(jnp.sum(gt * part, axis=0, keepdims=True))
        dots = jnp.concatenate(dots, axis=1)
        pltpu.make_async_copy(
            outbuf.at[s],
            out_hbm.at[rows(s * STRETCH, STRETCH, STRETCH)], out_sem.at[s],
        ).start()

        for j in range(REACH):
            at = pl.ds(j * STRETCH, STRETCH)
            w = wbuf[s, at, :].astype(jnp.float32)
            wbuf[s, at, :] = (w * (st[at, :] - dots)).astype(jnp.bfloat16)

        contrib_k[pl.ds(s * REACH, REACH)] = (
            dot(wbuf[s], qcat[s], nn) * scale
        ).reshape(REACH, STRETCH, HD)

    def query_side(s):
        for j in range(REACH):
            kt[:, pl.ds(j * STRETCH, STRETCH)] = kbuf[slots[s * REACH + j]].T
        dqt = dot(kt[...], wbuf[s], nn) * scale
        for h in range(4):
            dqbuf[pl.ds(s * per, per), :, pl.ds(h * HD, HD)] = dqt[
                :, h * HD:(h + 1) * HD
            ].T.reshape(per, short, HD).astype(jnp.bfloat16)

        @pl.loop(0, per)
        def _(i):
            b = s * per + i

            def remote():
                dq_copy(b, head, b).start()

            def own():
                dqrecv[head] = dqbuf[b]

            pl.when(b != head)(remote)
            pl.when(b == head)(own)

    def dq_copy(b, src, to):
        return pltpu.make_async_remote_copy(
            src_ref=dqbuf.at[b], dst_ref=dqrecv.at[src],
            send_sem=dq_send.at[b], recv_sem=dq_recv.at[src],
            device_id={"head": to}, device_id_type=pl.DeviceIdType.MESH,
        )

    contribs = (contrib_k, contrib_v)
    parts = (part_k, part_v)
    sibs = (sib_k, sib_v)

    def build(t, at):
        @pl.loop(0, 4)
        def _(k):
            here = order[at * 4 + k]
            total = None
            for s in range(4):
                delta = order[ctx * 4 + s] - here
                index = jnp.where(
                    (delta >= 0) & (delta < REACH), s * REACH + REACH - 1 - delta, 4 * REACH
                )
                term = contribs[t][index]
                total = term if total is None else total + term
            parts[t][at * 4 + k] = total.astype(jnp.bfloat16)

    def rs_copy(t, src, dst_, sem, device):
        return pltpu.make_async_remote_copy(
            src_ref=src, dst_ref=dst_, send_sem=rs_send.at[t, sem], recv_sem=rs_recv.at[t, sem],
            device_id=device, device_id_type=pl.DeviceIdType.MESH,
        )

    def rs_wait(t, ref, sem):
        rs_copy(t, ref, ref, sem, up).wait_recv()

    def dest(i):
        return zmod(z + far + ((i + 1) // 2) * (2 * lax.rem(i, 2) - 1))

    def rs_build(t):
        @pl.loop(0, nz)
        def _(i):
            rs_dest(t, i)

    def rs_dest(t, i):
        zt = dest(i)
        other = zt * 2 + 1 - core
        build(t, other)
        rs_copy(
            t, parts[t].at[pl.ds(other * 4, 4)], sibs[t].at[pl.ds(i * 4, 4)], RS_S + i, sib
        ).start()
        build(t, zt * 2 + core)

    def place(i):
        if i == nz - 1:
            return z
        delta = far + ((i + 1) // 2) * (2 * (i % 2) - 1)
        return zmod(z + delta)

    def chip_sum(t, i, start, size):
        return (
            parts[t][pl.ds((place(i) * 2 + core) * 4 + start, size)].astype(jnp.float32)
            + sibs[t][pl.ds(i * 4 + start, size)].astype(jnp.float32)
        )

    def own_x(t, i):
        rs_wait(t, yrecv.at[t, i], RS_Y + i)
        return chip_sum(t, i, x0, 1)[0] + yrecv[t, i].astype(jnp.float32)

    def own(t, u, i):
        return own_x(t, i) if u == 0 else chip_sum(t, i, u, 1)[0]

    def rs_chain(t, way, u, k):
        sem, first = chain(way, u), far + 1 - hops(way, u)
        c = way * 3 + u
        i = 2 * (k - 1) if way == UP else max(0, 2 * k - 3)
        if k > first:
            rs_wait(t, ring_in.at[t, c, k - 1], sem + k - 2)
        total = own(t, u, i)
        if k > first:
            total = total + ring_in[t, c, k - 1].astype(jnp.float32)
        ring_out[t, c, k] = total.astype(jnp.bfloat16)
        rs_copy(
            t, ring_out.at[t, c, k], ring_in.at[t, c, k], sem + k - 1, (up, down)[way]
        ).start()

    def rs_begin(t):
        for i in range(nz):
            rs_wait(t, sibs[t].at[pl.ds(i * 4, 4)], RS_S + i)
            ysend[t, i] = chip_sum(t, i, ox0, 1)[0].astype(jnp.bfloat16)
            rs_copy(t, ysend.at[t, i], yrecv.at[t, i], RS_Y + i, partner).start()
            if i == 0:
                rs_chain(t, DOWN, 1, 1)
                rs_chain(t, DOWN, 2, 1)
            if i == 2:
                rs_chain(t, UP, 1, 2)
                rs_chain(t, UP, 2, 2)

    def rs_begin_x(t):
        rs_chain(t, UP, 0, 1)
        rs_chain(t, DOWN, 0, 2)

    def rs_step(t, k):
        for way, u in ORDER:
            if k > far + 1 - hops(way, u):
                rs_chain(t, way, u, k)

    b0 = par * (XROWS // short)
    nb = ring_rows // short
    own_in = (head >= b0) & (head < b0 + nb)

    def fin_copy(t, b, src):
        return pltpu.make_async_remote_copy(
            src_ref=fin.at[t, rows(b * short, short)], dst_ref=finrecv.at[t, src],
            send_sem=fin_send.at[t, b], recv_sem=fin_recv.at[t, src],
            device_id={"head": b}, device_id_type=pl.DeviceIdType.MESH,
        )

    def rs_final(t):
        for u in range(3):
            total = own(t, u, nz - 1)
            for way in (UP, DOWN):
                c = way * 3 + u
                rs_wait(t, ring_in.at[t, c, far], chain(way, u) + far - 1)
                total = total + ring_in[t, c, far].astype(jnp.float32)
            fin[t, rows(at_unit(u) * STRETCH, STRETCH), :] = total.astype(jnp.bfloat16)

        @pl.loop(0, nb)
        def _(i):
            b = b0 + i
            pl.when(b != head)(lambda: fin_copy(t, b, head).start())

            def keep():
                finrecv[t, head] = fin[t, rows(head * short, short), :]

            pl.when(b == head)(keep)

    def rs_out(t, ref):
        @pl.loop(0, nh)
        def _(src):
            p = lax.rem(src, 2)
            sends = ((p == 0) & (head < last_b)) | ((p == 1) & (head >= first_b))
            pl.when(sends & (src != head))(lambda: fin_copy(t, 0, src).wait_recv())

        for g in range(nh // 2):
            ref[:, g * HD:(g + 1) * HD] = (
                finrecv[t, 2 * g].astype(jnp.float32) + finrecv[t, 2 * g + 1].astype(jnp.float32)
            ).astype(jnp.bfloat16)

    ag_first(0)
    ag_first(1)
    ag_step(0, 1)
    ag_step(1, 1)
    ag_step(0, 2)
    ag_step(1, 2)
    ag_step(0, 3)
    ag_step(1, 3)
    ag_step(0, 4)
    ag_finish(0)
    for n, s, h in heads:
        load_qg(n, s, h).wait()

    @pl.loop(0, 4)
    def _(s):
        scores(s)
        pl.when(s < far - 3)(lambda: ag_half(1, s + 4, 0))
        softmax(s)
        pl.when(s < far - 3)(lambda: ag_half(1, s + 4, 1))

    rs_build(1)
    ag_finish(1)
    key_side(0)
    rs_begin(1)
    key_side(1)
    key_side(2)
    key_side(3)
    rs_build(0)
    rs_begin_x(1)
    rs_begin(0)
    rs_step(1, 2)
    query_side(0)
    rs_begin_x(0)
    rs_step(1, 3)
    query_side(1)
    rs_step(0, 2)
    rs_step(1, 4)
    query_side(2)
    rs_step(0, 3)
    rs_final(1)
    query_side(3)
    rs_step(0, 4)
    rs_out(1, dv_ref)
    rs_final(0)
    rs_out(0, dk_ref)

    @pl.loop(0, nh)
    def _(src):
        pl.when(src != head)(lambda: dq_copy(0, src, src).wait_recv())

    for src in range(nh):
        dq_ref[:, src * 4 * HD:(src + 1) * 4 * HD] = dqrecv[src]
    @pl.loop(0, nh)
    def _(b):
        pl.when(b != head)(lambda: dq_copy(b, head, b).wait_send())

    for s in range(4):
        pltpu.make_async_copy(
            outbuf.at[s], out_hbm.at[pl.ds(s * STRETCH, STRETCH)], out_sem.at[s]
        ).wait()
    for t in range(2):
        chains = [(chain(w, u) + far - hops(w, u), hops(w, u)) for w, u in ORDER]
        for first, count, size in [(chain(w, u), hops(w, u), 1) for w, u in ORDER] + [
            (AG_Y, far, 1), (AG_Y + 4, far - 1, 1), (AG_SR, nz, 3), (AG_SO, nz, 1),
        ]:

            @pl.loop(first, first + count)
            def _(sem):
                ag_copy(t, z, 0, size, sem, up).wait_send()

        for first, count, ref in [(f, n, yrecv.at[t, 0]) for f, n in chains] + [
            (RS_S, nz, sibs[t].at[pl.ds(0, 4)]), (RS_Y, nz, yrecv.at[t, 0]),
        ]:

            @pl.loop(first, first + count)
            def _(sem):
                rs_copy(t, ref, ref, sem, up).wait_send()

        @pl.loop(0, nb)
        def _(i):
            pl.when(b0 + i != head)(lambda: fin_copy(t, b0 + i, head).wait_send())


def on_device(query_states, key_states, value_states, out_grad, stretch_order, doc_blocks):
    nz = lax.axis_size("ctx") // 2
    nh = lax.axis_size("head")
    far = nz // 2
    local = 4 * STRETCH
    crows = local - 2 * XROWS
    short = local // nh
    seq = 2 * nz * local
    bf, f32 = jnp.bfloat16, jnp.float32
    anywhere = pl.BlockSpec(memory_space=pl.ANY)
    smem = pl.BlockSpec(memory_space=pltpu.SMEM)
    vmem = pl.BlockSpec(memory_space=pltpu.VMEM)
    V, D = pltpu.VMEM, pltpu.SemaphoreType.DMA
    results = pl.pallas_call(
        functools.partial(kernel, nz, nh),
        out_shape=(
            jax.ShapeDtypeStruct((local, 4 * HD), bf),
            jax.ShapeDtypeStruct((short, nh * 4 * HD), bf),
            jax.ShapeDtypeStruct((short, nh // 2 * HD), bf),
            jax.ShapeDtypeStruct((short, nh // 2 * HD), bf),
        ),
        in_specs=[smem, smem, anywhere, anywhere, anywhere, anywhere],
        out_specs=(anywhere, vmem, vmem, vmem),
        scratch_shapes=[
            V((seq // STRETCH, STRETCH, HD), bf), V((seq // STRETCH, STRETCH, HD), bf),
            V((4, 512, HD), bf), V((4, 512, HD), bf),
            V((1024, HD), bf), V((HD, 1024), bf),
            V((1024, 512), f32), V((4, 1024, 512), bf), V((1, 512), f32),
            V((4 * REACH + 1, STRETCH, HD), f32), V((4 * REACH + 1, STRETCH, HD), f32),
            V((seq // STRETCH, STRETCH, HD), bf), V((seq // STRETCH, STRETCH, HD), bf),
            V((nz * 4, STRETCH, HD), bf), V((nz * 4, STRETCH, HD), bf),
            V((2, nz, XROWS, HD), bf), V((2, nz, XROWS, HD), bf),
            V((2, 6, far + 1, STRETCH, HD), bf), V((2, 6, far + 1, STRETCH, HD), bf),
            V((2, local, HD), bf), V((2, nh, short, HD), bf),
            V((4, STRETCH, 4 * HD), bf), V((nh, short, 4 * HD), bf), V((nh, short, 4 * HD), bf),
            pltpu.SMEM((4 * REACH,), jnp.int32), pltpu.SMEM((4 * REACH,), f32),
            D((2, AG_N)), D((2, AG_N)), D((2, RS_N)), D((2, RS_N)),
            D((2, nh)), D((2, nh)), D((nh,)), D((nh,)), D((4, 16)), D((4,)),
        ],
        compiler_params=pltpu.CompilerParams(
            collective_id=0, has_side_effects=True, vmem_limit_bytes=56 * 1024 * 1024
        ),
        cost_estimate=pl.CostEstimate(
            flops=3_300_000_000, bytes_accessed=4_000_000, transcendentals=2_100_000
        ),
    )(stretch_order, doc_blocks, query_states, key_states, value_states, out_grad)
    return pl.pallas_call(
        settle,
        out_shape=tuple(jax.ShapeDtypeStruct(r.shape, r.dtype) for r in results),
        in_specs=[vmem] * 4,
        out_specs=(vmem,) * 4,
    )(*results)


def settle(*refs):
    for n in range(4):
        refs[4 + n][...] = refs[n][...]


def solution(mesh):
    in_specs = (P("ctx", "head"), P("ctx", None), P("ctx", None), P("ctx", "head"), P(), P())
    out_specs = (
        P("ctx", "head"),
        P(("ctx", "head"), None),
        P(("ctx", "head"), None),
        P(("ctx", "head"), None),
    )
    return jax.shard_map(
        on_device, mesh=mesh, in_specs=in_specs, out_specs=out_specs, check_vma=False
    )
```

time: 95.9 us -> 83.8 us (0.87)
  Pallas kernels: 90.8 us -> 82.2 us
  local copies, waits for them, and re-layouts: 4.28 us -> 0 us
    pallas_call x1, Pallas kernels: 90.8 us -> 80 us  [on_device(): pl.pallas_call(functools.partial(kernel, nz, nh), out_shape=(jax.ShapeDty...]
    unnamed x10 -> x0, local copies, waits for them, and re-layouts: 4.28 us -> none
    pallas_call x0 -> x1, Pallas kernels: none -> 2.24 us  [on_device(): pl.pallas_call(settle, out_shape=tuple((jax.ShapeDtypeStruct(r.shape, r.d...]
where the time goes in v2:
time: 83.8 us; the launch traced here: 82.9 us
  Pallas kernels  82.2 us (98%)
    pallas_call x1, Pallas kernels, on_device(): pl.pallas_call(functools.partial(kernel, nz, nh), out_shape=(jax.ShapeDty...  80 us
    pallas_call x1, Pallas kernels, on_device(): pl.pallas_call(settle, out_shape=tuple((jax.ShapeDtypeStruct(r.shape, r.d...  2.24 us

profile of v2, /device:TPU:8, one launch (start us, length us, event | category | flops | bytes accessed | tf_op | source)
XLA Modules:
  0.0 82.9 jit_solution(4384976916553159813)
XLA Ops:
  0.6 80.0 %shard_map.93 = (bf16[512,512]{1,0:T(8,128)(2,1)}, bf16[32,8192]{1,0:T(8,128)(2,1)}, bf16[32,1024]{1,0:T(8,128)(2,1)}, bf16[32,1024]{1,0:T(8,128)(2,1)}) custom-call(s32[64]{0:T(128)} %order.1, s32[16]{0:T(128)} %blocks.1, bf16[512,512]{1,0:T(8,128)(2,1)} %q_hbm.1, bf16[512,1024]{1,0:T(8,128)(2,1)} %k_hbm.1, bf16[512,1024]{1,0:T(8,128)(2,1)} %v_hbm.1, ...), custom_call_target="tpu_custom_call" | custom-call | flops 3300000000 | bytes 4000000 | tf_op jit(solution)/shard_map/pallas_call | solution.py:566
  80.6 2.2 %shard_map.94 = (bf16[512,512]{1,0:T(8,128)(2,1)}, bf16[32,8192]{1,0:T(8,128)(2,1)}, bf16[32,1024]{1,0:T(8,128)(2,1)}, bf16[32,1024]{1,0:T(8,128)(2,1)}) custom-call(bf16[512,512]{1,0:T(8,128)(2,1)} %get-tuple-element.8.refs_0_, bf16[32,8192]{1,0:T(8,128)(2,1)} %get-tuple-element.9.refs_1_, bf16[32,1024]{1,0:T(8,128)(2,1)} %get-tuple-element.10.refs_2_, ...), custom_call_target="tpu_custom_call" | custom-call | tf_op jit(solution)/shard_map/pallas_call | solution.py:599

commit v3 on v2

--- a/solution.py
+++ b/solution.py
@@ -511,7 +511,6 @@
     rs_step(0, 4)
     rs_out(1, dv_ref)
     rs_final(0)
-    rs_out(0, dk_ref)
 
     @pl.loop(0, nh)
     def _(src):
@@ -548,6 +547,8 @@
         @pl.loop(0, nb)
         def _(i):
             pl.when(b0 + i != head)(lambda: fin_copy(t, b0 + i, head).wait_send())
+
+    rs_out(0, dk_ref)
 
 
 def on_device(query_states, key_states, value_states, out_grad, stretch_order, doc_blocks):

time: 83.8 us -> 82.1 us (0.980)
  Pallas kernels: 82.2 us -> 80.5 us
    pallas_call x1, Pallas kernels: 80 us -> 78.3 us  [on_device(): pl.pallas_call(functools.partial(kernel, nz, nh), out_shape=(jax.ShapeDty...]
where the time goes in v3:
time: 82.1 us; the launch traced here: 81.2 us
  Pallas kernels  80.5 us (98%)
    pallas_call x1, Pallas kernels, on_device(): pl.pallas_call(functools.partial(kernel, nz, nh), out_shape=(jax.ShapeDty...  78.3 us
    pallas_call x1, Pallas kernels, on_device(): pl.pallas_call(settle, out_shape=tuple((jax.ShapeDtypeStruct(r.shape, r.d...  2.24 us

profile of v3, /device:TPU:8, one launch (start us, length us, event | category | flops | bytes accessed | tf_op | source)
XLA Modules:
  0.0 81.2 jit_solution(2809323296150963301)
XLA Ops:
  0.6 78.3 %shard_map.93 = (bf16[512,512]{1,0:T(8,128)(2,1)}, bf16[32,8192]{1,0:T(8,128)(2,1)}, bf16[32,1024]{1,0:T(8,128)(2,1)}, bf16[32,1024]{1,0:T(8,128)(2,1)}) custom-call(s32[64]{0:T(128)} %order.1, s32[16]{0:T(128)} %blocks.1, bf16[512,512]{1,0:T(8,128)(2,1)} %q_hbm.1, bf16[512,1024]{1,0:T(8,128)(2,1)} %k_hbm.1, bf16[512,1024]{1,0:T(8,128)(2,1)} %v_hbm.1, ...), custom_call_target="tpu_custom_call" | custom-call | flops 3300000000 | bytes 4000000 | tf_op jit(solution)/shard_map/pallas_call | solution.py:567
  78.9 2.2 %shard_map.94 = (bf16[512,512]{1,0:T(8,128)(2,1)}, bf16[32,8192]{1,0:T(8,128)(2,1)}, bf16[32,1024]{1,0:T(8,128)(2,1)}, bf16[32,1024]{1,0:T(8,128)(2,1)}) custom-call(bf16[512,512]{1,0:T(8,128)(2,1)} %get-tuple-element.8.refs_0_, bf16[32,8192]{1,0:T(8,128)(2,1)} %get-tuple-element.9.refs_1_, bf16[32,1024]{1,0:T(8,128)(2,1)} %get-tuple-element.10.refs_2_, ...), custom_call_target="tpu_custom_call" | custom-call | tf_op jit(solution)/shard_map/pallas_call | solution.py:600

commit v4 on v3

--- a/solution.py
+++ b/solution.py
@@ -17,7 +17,7 @@
 AG_Y, AG_SR, AG_SO, AG_N = 24, 32, 40, 48
 RS_S, RS_Y, RS_N = 24, 32, 40
 UP, DOWN = 0, 1
-ORDER = ((UP, 0), (DOWN, 1), (UP, 1), (DOWN, 2), (UP, 2), (DOWN, 0))
+ORDER = ((UP, 0), (DOWN, 0), (DOWN, 1), (UP, 1), (DOWN, 2), (UP, 2))
 
 
 def when(cond, fn):
@@ -421,7 +421,7 @@
         rs_chain(t, DOWN, 0, 2)
 
     def rs_step(t, k):
-        for way, u in ORDER:
+        for way, u in ORDER[:1] + ORDER[2:] + ORDER[1:2]:
             if k > far + 1 - hops(way, u):
                 rs_chain(t, way, u, k)
 
@@ -429,31 +429,29 @@
     nb = ring_rows // short
     own_in = (head >= b0) & (head < b0 + nb)
 
-    def fin_copy(t, b, src):
+    def fin_copy(t, b, src, u=0, i=0):
         return pltpu.make_async_remote_copy(
-            src_ref=fin.at[t, rows(b * short, short)], dst_ref=finrecv.at[t, src],
+            src_ref=fin.at[t, u, pl.ds(i * short, short)], dst_ref=finrecv.at[t, src],
             send_sem=fin_send.at[t, b], recv_sem=fin_recv.at[t, src],
             device_id={"head": b}, device_id_type=pl.DeviceIdType.MESH,
         )
 
     def rs_final(t):
-        for u in range(3):
+        for u in (1, 2, 0):
             total = own(t, u, nz - 1)
             for way in (UP, DOWN):
                 c = way * 3 + u
                 rs_wait(t, ring_in.at[t, c, far], chain(way, u) + far - 1)
                 total = total + ring_in[t, c, far].astype(jnp.float32)
-            fin[t, rows(at_unit(u) * STRETCH, STRETCH), :] = total.astype(jnp.bfloat16)
-
-        @pl.loop(0, nb)
-        def _(i):
-            b = b0 + i
-            pl.when(b != head)(lambda: fin_copy(t, b, head).start())
-
-            def keep():
-                finrecv[t, head] = fin[t, rows(head * short, short), :]
-
-            pl.when(b == head)(keep)
+            fin[t, u] = total.astype(jnp.bfloat16)
+            for i in range(per):
+                b = at_unit(u) * per + i
+
+                def keep(u=u, i=i):
+                    finrecv[t, head] = fin[t, u, pl.ds(i * short, short), :]
+
+                pl.when(b != head)(lambda u=u, i=i, b=b: fin_copy(t, b, head, u, i).start())
+                pl.when(b == head)(keep)
 
     def rs_out(t, ref):
         @pl.loop(0, nh)
@@ -584,7 +582,7 @@
             V((nz * 4, STRETCH, HD), bf), V((nz * 4, STRETCH, HD), bf),
             V((2, nz, XROWS, HD), bf), V((2, nz, XROWS, HD), bf),
             V((2, 6, far + 1, STRETCH, HD), bf), V((2, 6, far + 1, STRETCH, HD), bf),
-            V((2, local, HD), bf), V((2, nh, short, HD), bf),
+            V((2, 3, STRETCH, HD), bf), V((2, nh, short, HD), bf),
             V((4, STRETCH, 4 * HD), bf), V((nh, short, 4 * HD), bf), V((nh, short, 4 * HD), bf),
             pltpu.SMEM((4 * REACH,), jnp.int32), pltpu.SMEM((4 * REACH,), f32),
             D((2, AG_N)), D((2, AG_N)), D((2, RS_N)), D((2, RS_N)),

time: 82.1 us -> 82 us (level)
  no operation moved by 1% of the time
where the time goes in v4:
time: 82 us; the launch traced here: 81.1 us
  Pallas kernels  80.5 us (98%)
    pallas_call x1, Pallas kernels, on_device(): pl.pallas_call(functools.partial(kernel, nz, nh), out_shape=(jax.ShapeDty...  78.2 us
    pallas_call x1, Pallas kernels, on_device(): pl.pallas_call(settle, out_shape=tuple((jax.ShapeDtypeStruct(r.shape, r.d...  2.24 us

profile of v4, /device:TPU:8, one launch (start us, length us, event | category | flops | bytes accessed | tf_op | source)
XLA Modules:
  0.0 81.1 jit_solution(13706052280962715851)
XLA Ops:
  0.6 78.2 %shard_map.93 = (bf16[512,512]{1,0:T(8,128)(2,1)}, bf16[32,8192]{1,0:T(8,128)(2,1)}, bf16[32,1024]{1,0:T(8,128)(2,1)}, bf16[32,1024]{1,0:T(8,128)(2,1)}) custom-call(s32[64]{0:T(128)} %order.1, s32[16]{0:T(128)} %blocks.1, bf16[512,512]{1,0:T(8,128)(2,1)} %q_hbm.1, bf16[512,1024]{1,0:T(8,128)(2,1)} %k_hbm.1, bf16[512,1024]{1,0:T(8,128)(2,1)} %v_hbm.1, ...), custom_call_target="tpu_custom_call" | custom-call | flops 3300000000 | bytes 4000000 | tf_op jit(solution)/shard_map/pallas_call | solution.py:565
  78.9 2.2 %shard_map.94 = (bf16[512,512]{1,0:T(8,128)(2,1)}, bf16[32,8192]{1,0:T(8,128)(2,1)}, bf16[32,1024]{1,0:T(8,128)(2,1)}, bf16[32,1024]{1,0:T(8,128)(2,1)}) custom-call(bf16[512,512]{1,0:T(8,128)(2,1)} %get-tuple-element.8.refs_0_, bf16[32,8192]{1,0:T(8,128)(2,1)} %get-tuple-element.9.refs_1_, bf16[32,1024]{1,0:T(8,128)(2,1)} %get-tuple-element.10.refs_2_, ...), custom_call_target="tpu_custom_call" | custom-call | tf_op jit(solution)/shard_map/pallas_call | solution.py:598
